TPU v7x, 256 devices: a whole 4x4x8 slice. The times are simulated.
256 devices in a mesh: rep: 32 (over z_lo, x, core), tp: 8 (over z_hi, y).
Axes of the slice: x: 4, y: 4, z: 8 (z_hi: 2, z_lo: 4; z = z_hi * 4 + z_lo), core: 2. Of those that a mesh axis runs over, the one named last changes fastest.
Arguments:
- tokens: bfloat16 [16384, 8192], P('rep'), may hold values from -6 to 6
- w_query: bfloat16 [8192, 4096], P('rep', 'tp'), may hold values from -1 to 1
- w_key: bfloat16 [8192, 512], P('rep'), may hold values from -1 to 1
- value_weight: bfloat16 [8192, 512], P('rep'), may hold values from -0.0625 to 0.0625
- w_out: bfloat16 [4096, 8192], P('rep', 'tp'), may hold values from -0.09375 to 0.09375
Outputs:
- mixed: bfloat16 [16384, 8192], P('rep', 'tp')
All inputs are finite; a program needn't handle non-finite values.
Results may differ from a plain program's by a relative error of at most 0.011.
Values may be sent and summed in bfloat16 or wider, within the bound.
A program may use at most 128 MiB of HBM per device.

v0:
```python
import jax
import jax.numpy as jnp
from jax import lax
from jax.sharding import PartitionSpec as P

QUERY_HEADS = 32
KEY_VALUE_HEADS = 4
HEAD_DIMENSION = 128


def apply_rotary(field, head_size):
    rows = field.shape[0]
    heads = field.shape[1] // head_size
    shaped = field.reshape(rows, heads, head_size)
    positions = jnp.arange(rows, dtype=jnp.float32)
    freqs = 1000000.0 ** (-(jnp.arange(head_size // 2, dtype=jnp.float32) * 2.0 / head_size))
    angles = positions[:, None] * freqs[None, :]
    cosine = jnp.cos(angles)[:, None, :]
    sine = jnp.sin(angles)[:, None, :]
    first = shaped[:, :, : head_size // 2]
    second = shaped[:, :, head_size // 2 :]
    turned = jnp.concatenate(
        [first * cosine - second * sine, second * cosine + first * sine], axis=2
    )
    return turned.reshape(rows, heads * head_size)


def body(tokens, w_query, w_key, value_weight, w_out):
    rows = tokens.shape[0]
    head_size = HEAD_DIMENSION
    widened = tokens.astype(jnp.float32)
    scale = lax.rsqrt(jnp.mean(widened * widened, axis=1, keepdims=True) + 1e-06)
    normed = (widened * scale).astype(jnp.bfloat16)
    full_query, full_key, full_value = (
        lax.all_gather(w_query, "rep", axis=0, tiled=True),
        lax.all_gather(w_key, "rep", axis=0, tiled=True),
        lax.all_gather(value_weight, "rep", axis=0, tiled=True),
    )
    query_state = jnp.dot(normed, full_query, preferred_element_type=jnp.float32)
    key_rows = jnp.dot(normed, full_key, preferred_element_type=jnp.float32)
    value_state = jnp.dot(normed, full_value, preferred_element_type=jnp.float32)
    q_local = query_state.shape[1] // head_size
    group_total = QUERY_HEADS // KEY_VALUE_HEADS
    kv_local = max(1, q_local // group_total)
    first_head = lax.axis_index("tp") * q_local // group_total
    key_rows = lax.dynamic_slice_in_dim(key_rows, first_head * head_size, kv_local * head_size, 1)
    value_state = lax.dynamic_slice_in_dim(
        value_state, first_head * head_size, kv_local * head_size, 1
    )
    value_state = value_state.astype(jnp.bfloat16)
    query_state = apply_rotary(query_state, head_size).astype(jnp.bfloat16)
    key_rows = apply_rotary(key_rows, head_size).astype(jnp.bfloat16)
    group_index = q_local // kv_local
    query_head_rows = query_state.reshape(rows, kv_local, group_index, head_size)
    key_head_rows = key_rows.reshape(rows, kv_local, head_size)
    value_head_rows = value_state.reshape(rows, kv_local, head_size)
    block_rows = min(512, rows)
    scores = jnp.einsum(
        "qgjd,kgd->gjqk", query_head_rows, key_head_rows, preferred_element_type=jnp.float32
    )
    scores = scores / jnp.sqrt(jnp.float32(head_size))
    causal = jnp.arange(block_rows)[:, None] + 0 >= jnp.arange(rows)[None, :]
    scores = jnp.where(causal[None, None], scores, jnp.float32(-1e30))
    top = jnp.max(scores, axis=3, keepdims=True)
    expo = jnp.exp(scores - top)
    weights = (expo / jnp.sum(expo, axis=3, keepdims=True)).astype(jnp.bfloat16)
    part_heads = jnp.einsum(
        "gjqk,kgd->qgjd", weights, value_head_rows, preferred_element_type=jnp.float32
    )
    outputs = part_heads.reshape(block_rows, q_local * head_size).astype(jnp.bfloat16)
    all_heads = lax.all_gather(outputs, "tp", axis=1, tiled=True)
    projected = jnp.dot(
        all_heads,
        lax.all_gather(w_out, "rep", axis=0, tiled=True),
        preferred_element_type=jnp.float32,
    )
    width = w_out.shape[1]
    residual = lax.dynamic_slice_in_dim(widened, lax.axis_index("tp") * width, width, 1)
    return (residual + projected).astype(jnp.bfloat16)


def solution(mesh):
    placed = (P("rep", None), P("rep", "tp"), P("rep", None), P("rep", None), P("rep", "tp"))
    return jax.shard_map(
        body, mesh=mesh, in_specs=placed, out_specs=P("rep", "tp"), check_vma=False
    )
```

profile of v0, /device:TPU:1, one launch (start us, length us, event | category | flops | bytes accessed | tf_op | source)
XLA Modules:
  0.0 416.6 jit_solution(4376140013780937415)
XLA Ops:
  6.5 0.7 all-gather.8.cloned.1.call-update
  7.3 0.7 all-gather.10.cloned.1.call-update
  8.1 0.7 all-gather.6.cloned.1.call-update
  8.8 0.5 all-gather.14.cloned.1.call-update
  9.5 5.1 %multiply_reduce_fusion = f32[512]{0:T(512)S(1)} fusion(bf16[512,8192]{1,0:T(8,128)(2,1)} %param.5), kind=kLoop, calls=%fused_computation.1 | loop fusion | flops 12582400 | bytes 8390656 | tf_op jit(solution)/shard_map/reduce_sum | solution.py:32
  14.6 1.7 fusion.13
  16.3 66.3 %all-gather.8.cloned.1.call-done = bf16[8192,512]{1,0:T(8,128)(2,1)} async-done(((bf16[256,512]{1,0:T(8,128)(2,1)}), bf16[8192,512]{1,0:T(8,128)(2,1)}) %all-gather.8.cloned.1.call-update) | async-done | bytes 8388624 | tf_op jit(solution)/shard_map/all_gather | solution.py:36
  82.6 9.9 %fusion.27 = f32[512,512]{0,1:T(8,128)S(1)} fusion(bf16[8192,512]{1,0:T(8,128)(2,1)} %all-gather.8.cloned.1.call-done, f32[512]{0:T(512)S(1)} %add_rsqrt_fusion, bf16[512,8192]{1,0:T(8,128)(2,1)} %param.5), kind=kOutput, calls=%fused_computation.42 | convolution fusion | flops 4307550208 | bytes 17827840 | tf_op jit(solution)/shard_map/dot_general | solution.py:40
  92.7 59.7 %all-gather.10.cloned.1.call-done = bf16[8192,512]{1,0:T(8,128)(2,1)} async-done(((bf16[256,512]{1,0:T(8,128)(2,1)}), bf16[8192,512]{1,0:T(8,128)(2,1)}) %all-gather.10.cloned.1.call-update) | async-done | bytes 8388624 | tf_op jit(solution)/shard_map/all_gather | solution.py:35
  152.4 9.9 %fusion.26 = f32[512,512]{0,1:T(8,128)S(1)} fusion(bf16[8192,512]{1,0:T(8,128)(2,1)} %all-gather.10.cloned.1.call-done, f32[512]{0:T(512)S(1)} %add_rsqrt_fusion, bf16[512,8192]{1,0:T(8,128)(2,1)} %param.5), kind=kOutput, calls=%fused_computation.41 | convolution fusion | flops 4307550208 | bytes 17827840 | tf_op jit(solution)/shard_map/dot_general | solution.py:39
  162.4 0.3 copy.14
  162.8 0.3 copy.15
  163.1 1.3 fusion.20
  164.4 1.3 subtract_convert_fusion
  165.7 1.2 fusion.1
  167.0 2.0 copy-done
  168.9 0.9 fusion
  169.8 52.4 %all-gather.6.cloned.1.call-done = bf16[8192,512]{1,0:T(8,128)(2,1)} async-done(((bf16[256,512]{1,0:T(8,128)(2,1)}), bf16[8192,512]{1,0:T(8,128)(2,1)}) %all-gather.6.cloned.1.call-update) | async-done | bytes 8388624 | tf_op jit(solution)/shard_map/all_gather | solution.py:37
  222.3 11.3 %fusion.28 = bf16[512,512]{0,1:T(8,128)(2,1)} fusion(bf16[8192,512]{1,0:T(8,128)(2,1)} %all-gather.6.cloned.1.call-done, f32[512]{0:T(512)S(1)} %add_rsqrt_fusion, bf16[512,8192]{1,0:T(8,128)(2,1)} %param.5), kind=kOutput, calls=%fused_computation.43 | convolution fusion | flops 4307550208 | bytes 17303552 | tf_op jit(solution)/shard_map/dot_general | solution.py:41
  233.6 3.3 fusion.5
  236.8 11.6 %convert_element_type.33 = f32[512,8192]{1,0:T(8,128)} convert(bf16[512,8192]{1,0:T(8,128)(2,1)} %param.5) | non-fusion elementwise | flops 4194304 | bytes 25165824 | tf_op jit(solution)/shard_map/convert_element_type | solution.py:31
  248.4 43.8 %all-gather.14.cloned.1.call-done = bf16[4096,1024]{1,0:T(8,128)(2,1)} async-done(((bf16[128,1024]{1,0:T(8,128)(2,1)}), bf16[4096,1024]{1,0:T(8,128)(2,1)}) %all-gather.14.cloned.1.call-update) | async-done | bytes 8388624 | tf_op jit(solution)/shard_map/all_gather | solution.py:74
  292.2 107.2 %all-gather.12.cloned.1.call-done = bf16[512,4096]{0,1:T(8,128)(2,1)} async-done(((bf16[512,512]{0,1:T(8,128)(2,1)}), bf16[512,4096]{0,1:T(8,128)(2,1)}) %all-gather.12.cloned.1.call-update) | async-done | bytes 4194320 | tf_op jit(solution)/shard_map/all_gather | solution.py:71
  399.4 10.6 %add_convert_fusion = bf16[512,1024]{1,0:T(8,128)(2,1)} fusion(f32[512,8192]{1,0:T(8,128)} %convert_element_type.33, s32[]{:T(128)S(6)} %select_n.16, bf16[512,4096]{0,1:T(8,128)(2,1)} %all-gather.12.cloned.1.call-done, bf16[4096,1024]{1,0:T(8,128)(2,1)} %all-gather.14.cloned.1.call-done), kind=kOutput, calls=%fused_computation.9 | convolution fusion | flops 4296015872 | bytes 15728644 | tf_op jit(solution)/shard_map/dot_general | solution.py:72
  (15 shorter events, 0.5 us)
Async XLA Ops:
  6.5 76.1 %all-gather.8.cloned.1.call-start = ((), (), s32[]{:S(2)}) async-start(), calls=%async_computation.1 | async-start | bytes 8650752 | tf_op jit(solution)/shard_map/all_gather | solution.py:36
  7.3 145.2 %all-gather.10.cloned.1.call-start = ((), (), s32[]{:S(2)}) async-start(), calls=%async_computation.2 | async-start | bytes 8650752 | tf_op jit(solution)/shard_map/all_gather | solution.py:35
  8.0 214.2 %all-gather.6.cloned.1.call-start = ((), (), s32[]{:S(2)}) async-start(), calls=%async_computation | async-start | bytes 8650752 | tf_op jit(solution)/shard_map/all_gather | solution.py:37
  8.7 283.5 %all-gather.14.cloned.1.call-start = ((), (), s32[]{:S(2)}) async-start(), calls=%async_computation.4 | async-start | bytes 8650752 | tf_op jit(solution)/shard_map/all_gather | solution.py:74
  9.3 390.1 %all-gather.12.cloned.1.call-start = ((), (), s32[]{:S(2)}) async-start(), calls=%async_computation.3 | async-start | bytes 4718592 | tf_op jit(solution)/shard_map/all_gather | solution.py:71
  166.9 2.0 copy-start
  222.3 11.3 %copy-start.1 = (f32[512,512,4]{1,0,2:T(8,128)S(1)}, f32[512,512,4]{1,0,2:T(8,128)}, u32[]{:S(2)}) copy-start(f32[512,512,4]{1,0,2:T(8,128)} %copy-done) | copy-start | bytes 12582916
Sparse Core Ops, SparseCore 0:
  9.2 73.3 all-gather.7
  84.5 67.9 all-gather.9
  154.3 67.9 all-gather.5
  224.0 68.2 all-gather.13
  294.7 104.6 all-gather.11
where the time goes:
time: 417 us
  waiting for transfers between devices  332 us (80%)
  matrix products  46.3 us (11%)
  other arithmetic  22 us (5%)
  between operations  13.3 us (3%)
    all_gather x1, waiting for transfers between devices, body(): all_heads = lax.all_gather(outputs, 'tp', axis=1, tiled=True)  107 us
    all_gather x1, waiting for transfers between devices, body(): lax.all_gather(w_key, 'rep', axis=0, tiled=True)  66.3 us
    all_gather x1, waiting for transfers between devices, body(): lax.all_gather(w_query, 'rep', axis=0, tiled=True)  59.7 us
    all_gather x1, waiting for transfers between devices, body(): lax.all_gather(value_weight, 'rep', axis=0, tiled=True)  52.4 us
    all_gather x1, waiting for transfers between devices, body(): lax.all_gather(w_out, 'rep', axis=0, tiled=True)  43.8 us
    convert_element_type x1, other arithmetic, body(): widened = tokens.astype(jnp.float32)  11.6 us
    dot_general x1, matrix products, body(): jnp.dot(normed, full_value, preferred_element_type=jnp.float32)  11.3 us
    dot_general x1, matrix products, body(): jnp.dot(all_heads, lax.all_gather(w_out, 'rep', axis=0, tiled=True), pref...  10.6 us
  transfers between devices with their start and end apart: 5, of which 5 were waited for; matrix products, arithmetic and copies ran while one was open for 14% of the time, Pallas kernels for 0%

commit v1 on v0

v1 whole, which is shorter than its diff:
```python
import functools

import jax
import jax.numpy as jnp
import numpy as np
from jax import lax
from jax.experimental import pallas as pl
from jax.experimental.pallas import tpu as pltpu
from jax.sharding import PartitionSpec as P

MESH = pl.DeviceIdType.MESH
HEAD = 128
TOK = 512
WIDTH = 8192
FEATURES = 4096
HEADS = 4
OUT_COLS = 256
OUT_CHUNKS = 4
CHUNKS = 1 + HEADS + OUT_CHUNKS
SEMS = 160


def rotary_tables():
    pos = np.arange(TOK, dtype=np.float32)
    freqs = (1000000.0 ** (-(np.arange(HEAD // 2, dtype=np.float64) * 2.0 / HEAD))).astype(np.float32)
    angles = (pos[:, None] * freqs[None, :]).astype(np.float32).astype(np.float64)
    cosine, sine = np.cos(angles), np.sin(angles)
    return (
        np.concatenate([cosine, cosine], axis=1).astype(np.float32),
        np.concatenate([-sine, sine], axis=1).astype(np.float32),
    )


def kernel(tok_hbm, wq_hbm, wk_hbm, wv_hbm, wo_hbm, cos_hbm, sin_hbm, out_hbm,
           tok, wkv, wq, wo, heads, kv, res, cosv, sinv, outv, scale, ss, rs, ls):
    r = lax.axis_index("rep")
    t = lax.axis_index("tp")
    c, x, z = lax.rem(r, 2), lax.rem(lax.div(r, 2), 4), lax.div(r, 8)
    y, zh = lax.rem(t, 4), lax.div(t, 4)

    def at(z_, x_, c_):
        return ((z_ * 4 + x_) * 2 + c_, t)

    def at_tp(zh_, y_):
        return (r, zh_ * 4 + y_)

    def mod4(v):
        return lax.rem(v, 4)

    right, left, far = mod4(x + 1), mod4(x + 3), mod4(x + 2)
    sibling = at(z, x, 1 - c)
    to_right, to_left = at(z, right, c), at(z, left, c)
    z_peers = [at(mod4(z + d), x, c) for d in (1, 2, 3)]
    y_peers = [at_tp(zh, mod4(y + d)) for d in (1, 3, 2)]
    opposite = at_tp(1 - zh, y)
    parity = lax.rem(y, 2)
    y_pair = at_tp(zh, y + 1 - 2 * parity)

    def buf(k):
        if k == 0:
            return wkv
        if k <= HEADS:
            return wq.at[k - 1]
        return wo.at[k - 1 - HEADS]

    kv_col = pl.multiple_of(lax.div(t, 2) * HEAD, HEAD)
    own = []
    for k in range(CHUNKS):
        dst = buf(k).at[z, x, c]
        if k == 0:
            copy_k = pltpu.make_async_copy(wk_hbm.at[:, pl.ds(kv_col, HEAD)], dst, ls.at[0])
            copy_v = pltpu.make_async_copy(wv_hbm.at[:, pl.ds(kv_col, HEAD)], dst, ls.at[0])
            pl.when(parity == 0)(copy_k.start)
            pl.when(parity == 1)(copy_v.start)
            own.append(copy_k)
            continue
        if k <= HEADS:
            src = wq_hbm.at[:, pl.ds((k - 1) * HEAD, HEAD)]
        else:
            src = wo_hbm.at[:, pl.ds((k - 1 - HEADS) * OUT_COLS, OUT_COLS)]
        copy = pltpu.make_async_copy(src, dst, ls.at[k])
        copy.start()
        own.append(copy)
    load_tok = pltpu.make_async_copy(tok_hbm, tok, ls.at[CHUNKS])
    load_tok.start()
    res_col = pl.multiple_of(t * (OUT_COLS * OUT_CHUNKS), OUT_COLS)
    load_res = pltpu.make_async_copy(
        tok_hbm.at[:, pl.ds(res_col, OUT_COLS * OUT_CHUNKS)], res, ls.at[CHUNKS + 1]
    )
    load_cos = pltpu.make_async_copy(cos_hbm, cosv, ls.at[CHUNKS + 2])
    load_sin = pltpu.make_async_copy(sin_hbm, sinv, ls.at[CHUNKS + 3])
    for copy in (load_res, load_cos, load_sin):
        copy.start()

    barrier = pltpu.get_barrier_semaphore()
    partners = [sibling, to_right, to_left, *z_peers, *y_peers, opposite]
    for partner in partners:
        pl.semaphore_signal(barrier, inc=1, device_id=partner, device_id_type=MESH)
    pl.semaphore_wait(barrier, len(partners))

    sent = []

    def send(src, dst, device):
        i = len(sent)
        copy = pltpu.make_async_remote_copy(
            src_ref=src, dst_ref=dst, send_sem=ss.at[i], recv_sem=rs.at[i],
            device_id=device, device_id_type=MESH,
        )
        copy.start()
        sent.append(copy)
        return copy

    along_z, along_x, forwarded, across = {}, {}, {}, {}

    def z_send(k):
        own[k].wait()
        block = buf(k).at[z, x, c]
        along_z[k] = [send(block, block, peer) for peer in z_peers]

    def x_send(k):
        for copy in along_z[k]:
            copy.wait_recv()
        column = buf(k).at[:, x, c]
        along_x[k] = [send(column, column, to_right), send(column, column, to_left)]
        across[k] = [send(column, column, sibling)]

    def x_forward(k):
        from_left, from_right = buf(k).at[:, left, c], buf(k).at[:, right, c]
        along_x[k][0].wait_recv()
        low = buf(k).at[pl.ds(0, 2), left, c]
        forwarded[k] = [send(low, low, to_right)]
        across[k].append(send(from_left, from_left, sibling))
        along_x[k][1].wait_recv()
        high = buf(k).at[pl.ds(2, 2), right, c]
        forwarded[k].append(send(high, high, to_left))
        across[k].append(send(from_right, from_right, sibling))

    def finish(k):
        for copy in forwarded[k]:
            copy.wait_recv()
        last = buf(k).at[:, far, c]
        across[k].append(send(last, last, sibling))

    def arrived(k):
        for copy in across[k]:
            copy.wait_recv()

    def rotate(field):
        return field * cosv[...] + pltpu.roll(field, HEAD // 2, 1) * sinv[...]

    def statistics():
        load_tok.wait()

        @pl.loop(0, TOK // 32)
        def _(i):
            rows = pl.ds(pl.multiple_of(i * 32, 32), 32)
            wide = tok[rows, :].astype(jnp.float32)
            mean = jnp.sum(wide * wide, axis=1, keepdims=True) * (1.0 / WIDTH)
            scale[rows, :] = jnp.broadcast_to(lax.rsqrt(mean + 1e-6), (32, HEAD))

    def project(weights):
        product = jnp.dot(
            tok[...], weights[...].reshape(WIDTH, HEAD), preferred_element_type=jnp.float32
        )
        return product * scale[...]

    pair = []

    def key_or_value():
        for copy in (load_cos, load_sin):
            copy.wait()
        field = project(wkv)
        kv[parity] = jnp.where(parity == 0, rotate(field), field).astype(jnp.bfloat16)
        pair.append(send(kv.at[parity], kv.at[parity], y_pair))

    def head_block(zh_, y_, h):
        col = pl.multiple_of(((zh_ * 4 + y_) * HEADS + h) * HEAD, HEAD)
        return heads.at[:, pl.ds(col, HEAD)]

    near_heads, far_heads = {}, {}

    def attend(h):
        query = rotate(project(wq.at[h])).astype(jnp.bfloat16)
        if h == 0:
            pair[0].wait_recv()
        step = 128
        for i in range(TOK // step):
            extent = (i + 1) * step
            rows = query[i * step : extent, :]
            scores = lax.dot_general(
                rows, kv[0, :extent, :], (((1,), (1,)), ((), ())),
                preferred_element_type=jnp.float32,
            ) * (HEAD ** -0.5)
            q_pos = lax.broadcasted_iota(jnp.int32, (step, extent), 0) + i * step
            k_pos = lax.broadcasted_iota(jnp.int32, (step, extent), 1)
            scores = jnp.where(q_pos >= k_pos, scores, -1e30)
            expo = jnp.exp(scores - jnp.max(scores, axis=1, keepdims=True))
            weights = (expo / jnp.sum(expo, axis=1, keepdims=True)).astype(jnp.bfloat16)
            part = jnp.dot(weights, kv[1, :extent, :], preferred_element_type=jnp.float32)
            col = pl.multiple_of((t * HEADS + h) * HEAD, HEAD)
            heads[pl.ds(i * step, step), pl.ds(col, HEAD)] = part.astype(jnp.bfloat16)
        block = head_block(zh, y, h)
        near_heads[h] = [send(block, block, opposite)]
        near_heads[h] += [send(block, block, peer) for peer in y_peers]

    def pass_on(h):
        near_heads[h][0].wait_recv()
        block = head_block(1 - zh, y, h)
        far_heads[h] = [send(block, block, peer) for peer in y_peers]

    def gather_heads():
        for h in range(HEADS):
            for copy in near_heads[h][1:] + far_heads[h]:
                copy.wait_recv()

    stores = []

    def output(j):
        product = jnp.dot(
            heads[...], wo[j].reshape(FEATURES, OUT_COLS), preferred_element_type=jnp.float32
        )
        cols = pl.ds(j * OUT_COLS, OUT_COLS)
        outv[:, cols] = (res[:, cols].astype(jnp.float32) + product).astype(jnp.bfloat16)
        store = pltpu.make_async_copy(outv.at[:, cols], out_hbm.at[:, cols], ls.at[CHUNKS + 4 + j])
        store.start()
        stores.append(store)

    for k in range(3):
        z_send(k)
    x_send(0)
    statistics()
    x_send(1)
    for k in range(CHUNKS + 1):
        if k < CHUNKS:
            x_forward(k)
        if k + 3 < CHUNKS:
            z_send(k + 3)
        if k + 2 < CHUNKS:
            x_send(k + 2)
        if k >= 1:
            finish(k - 1)
            arrived(k - 1)
            if k - 1 == 0:
                key_or_value()
            elif k - 1 <= HEADS:
                h = k - 2
                attend(h)
                if h >= 1:
                    pass_on(h - 1)
            else:
                j = k - 2 - HEADS
                if j == 0:
                    pass_on(HEADS - 1)
                    load_res.wait()
                if j == 1:
                    gather_heads()
                    output(0)
                if j >= 1:
                    output(j)
    for copy in sent:
        copy.wait_send()
    for store in stores:
        store.wait()


def body(tokens, w_query, w_key, value_weight, w_out):
    cosine, sine = rotary_tables()
    any_space = pl.BlockSpec(memory_space=pl.ANY)
    blocks = (4, 4, 2)
    return pl.pallas_call(
        kernel,
        out_shape=jax.ShapeDtypeStruct((TOK, OUT_COLS * OUT_CHUNKS), jnp.bfloat16),
        in_specs=[any_space] * 7,
        out_specs=any_space,
        scratch_shapes=[
            pltpu.VMEM((TOK, WIDTH), jnp.bfloat16),
            pltpu.VMEM((*blocks, 256, HEAD), jnp.bfloat16),
            pltpu.VMEM((HEADS, *blocks, 256, HEAD), jnp.bfloat16),
            pltpu.VMEM((OUT_CHUNKS, *blocks, 128, OUT_COLS), jnp.bfloat16),
            pltpu.VMEM((TOK, FEATURES), jnp.bfloat16),
            pltpu.VMEM((2, TOK, HEAD), jnp.bfloat16),
            pltpu.VMEM((TOK, OUT_COLS * OUT_CHUNKS), jnp.bfloat16),
            pltpu.VMEM((TOK, HEAD), jnp.float32),
            pltpu.VMEM((TOK, HEAD), jnp.float32),
            pltpu.VMEM((TOK, OUT_COLS * OUT_CHUNKS), jnp.bfloat16),
            pltpu.VMEM((TOK, HEAD), jnp.float32),
            pltpu.SemaphoreType.DMA((SEMS,)),
            pltpu.SemaphoreType.DMA((SEMS,)),
            pltpu.SemaphoreType.DMA((CHUNKS + 4 + OUT_CHUNKS,)),
        ],
        compiler_params=pltpu.CompilerParams(
            collective_id=0, has_side_effects=True, vmem_limit_bytes=60 * 2**20
        ),
        cost_estimate=pl.CostEstimate(flops=11 * 10**9, bytes_accessed=12 * 2**20, transcendentals=2**20),
    )(tokens, w_query, w_key, value_weight, w_out, jnp.asarray(cosine), jnp.asarray(sine))


def solution(mesh):
    placed = (P("rep", None), P("rep", "tp"), P("rep", None), P("rep", None), P("rep", "tp"))
    return jax.shard_map(
        body, mesh=mesh, in_specs=placed, out_specs=P("rep", "tp"), check_vma=False
    )
```

time: 417 us -> 129 us (0.31)
  the two profiles are of different devices: /device:TPU:1 before, /device:TPU:97 now
where the time goes in v1:
time: 129 us; the launch traced here: 128 us
  Pallas kernels  126 us (98%)
  local copies, waits for them, and re-layouts  2.26 us (2%)
    pallas_call x1, Pallas kernels, body(): pl.pallas_call(kernel, out_shape=jax.ShapeDtypeStruct((TOK, OUT_COLS * OU...  126 us

profile of v1, /device:TPU:97, one launch (start us, length us, event | category | flops | bytes accessed | tf_op | source)
XLA Modules:
  0.0 128.5 jit_solution(2901711740738607204)
XLA Ops:
  0.0 126.2 %shard_map.73 = bf16[512,1024]{1,0:T(8,128)(2,1)} custom-call(bf16[512,8192]{1,0:T(8,128)(2,1)} %tok_hbm.1, bf16[256,512]{1,0:T(8,128)(2,1)} %wq_hbm.1, bf16[256,512]{1,0:T(8,128)(2,1)} %wk_hbm.1, bf16[256,512]{1,0:T(8,128)(2,1)} %wv_hbm.1, bf16[128,1024]{1,0:T(8,128)(2,1)} %wo_hbm.1, f32[512,128]{1,0:T(8,128)} %constant.4.clone.cos_hbm, ...), custom_call_target="tpu_custom_call" | custom-call | flops 11000000512 | bytes 12582912 | tf_op jit(solution)/shard_map/pallas_call | solution.py:270
  126.2 2.3 %copy.9 = bf16[512,1024]{1,0:T(8,128)(2,1)} copy(bf16[512,1024]{1,0:T(8,128)(2,1)} %shard_map.73) | data formatting | bytes 2097152

commit v2 on v1

v2 whole, which is shorter than its diff:
```python
import functools

import jax
import jax.numpy as jnp
import numpy as np
from jax import lax
from jax.experimental import pallas as pl
from jax.experimental.pallas import tpu as pltpu
from jax.sharding import PartitionSpec as P

MESH = pl.DeviceIdType.MESH
HEAD = 128
TOK = 512
WIDTH = 8192
FEATURES = 4096
HEADS = 4
OUT_COLS = 256
OUT_CHUNKS = 4
PAIR = 2 * HEAD
PAIRS = HEADS // 2
CHUNKS = 1 + PAIRS + OUT_CHUNKS
ROWS = 128
SEMS = 160


def rotary_tables():
    pos = np.arange(TOK, dtype=np.float32)
    freqs = (1000000.0 ** (-(np.arange(HEAD // 2, dtype=np.float64) * 2.0 / HEAD))).astype(np.float32)
    angles = (pos[:, None] * freqs[None, :]).astype(np.float32).astype(np.float64)
    cosine, sine = np.cos(angles), np.sin(angles)
    return (
        np.concatenate([cosine, cosine], axis=1).astype(np.float32),
        np.concatenate([-sine, sine], axis=1).astype(np.float32),
    )


def kernel(tok_hbm, wq_hbm, wk_hbm, wv_hbm, wo_hbm, cos_hbm, sin_hbm, out_hbm,
           tok, wkv, wq, wo, heads, query, kv, res, cosv, sinv, outv, scale, ss, rs, ls):
    r = lax.axis_index("rep")
    t = lax.axis_index("tp")
    c, x, z = lax.rem(r, 2), lax.rem(lax.div(r, 2), 4), lax.div(r, 8)
    y, zh = lax.rem(t, 4), lax.div(t, 4)

    def at(z_, x_, c_):
        return ((z_ * 4 + x_) * 2 + c_, t)

    def at_tp(zh_, y_):
        return (r, zh_ * 4 + y_)

    def mod4(v):
        return lax.rem(v, 4)

    right, left, far = mod4(x + 1), mod4(x + 3), mod4(x + 2)
    sibling = at(z, x, 1 - c)
    to_right, to_left = at(z, right, c), at(z, left, c)
    z_peers = [at(mod4(z + d), x, c) for d in (1, 2, 3)]
    y_peers = [at_tp(zh, mod4(y + d)) for d in (1, 3)]
    opposite = at_tp(1 - zh, y)
    parity = lax.rem(y, 2)
    y_pair = at_tp(zh, y + 1 - 2 * parity)
    def buf(k):
        if k == 0:
            return wkv
        if k <= PAIRS:
            return wq.at[k - 1]
        return wo.at[k - 1 - PAIRS]

    kv_col = pl.multiple_of(lax.div(t, 2) * HEAD, HEAD)
    own = []
    for k in range(CHUNKS):
        dst = buf(k).at[0, x, c]
        if k == 0:
            copy_k = pltpu.make_async_copy(wk_hbm.at[:, pl.ds(kv_col, HEAD)], dst, ls.at[0])
            copy_v = pltpu.make_async_copy(wv_hbm.at[:, pl.ds(kv_col, HEAD)], dst, ls.at[0])
            pl.when(parity == 0)(copy_k.start)
            pl.when(parity == 1)(copy_v.start)
            own.append(copy_k)
            continue
        if k <= PAIRS:
            src = wq_hbm.at[:, pl.ds((k - 1) * PAIR, PAIR)]
        else:
            src = wo_hbm.at[:, pl.ds((k - 1 - PAIRS) * OUT_COLS, OUT_COLS)]
        copy = pltpu.make_async_copy(src, dst, ls.at[k])
        copy.start()
        own.append(copy)
    load_tok = []
    for slot in range(4):
        part = WIDTH // 4
        col = pl.multiple_of(mod4(z + slot) * part, part)
        copy = pltpu.make_async_copy(
            tok_hbm.at[:, pl.ds(col, part)], tok.at[:, pl.ds(slot * part, part)], ls.at[CHUNKS + slot]
        )
        copy.start()
        load_tok.append(copy)
    res_col = pl.multiple_of(t * (OUT_COLS * OUT_CHUNKS), OUT_COLS)
    load_res = pltpu.make_async_copy(
        tok_hbm.at[:, pl.ds(res_col, OUT_COLS * OUT_CHUNKS)], res, ls.at[CHUNKS + 4]
    )
    load_cos = pltpu.make_async_copy(cos_hbm, cosv, ls.at[CHUNKS + 5])
    load_sin = pltpu.make_async_copy(sin_hbm, sinv, ls.at[CHUNKS + 6])
    for copy in (load_res, load_cos, load_sin):
        copy.start()

    barrier = pltpu.get_barrier_semaphore()
    partners = [sibling, to_right, to_left, *z_peers, *y_peers, opposite]
    for partner in partners:
        pl.semaphore_signal(barrier, inc=1, device_id=partner, device_id_type=MESH)
    pl.semaphore_wait(barrier, len(partners))

    sent = []

    def send(src, dst, device):
        i = len(sent)
        copy = pltpu.make_async_remote_copy(
            src_ref=src, dst_ref=dst, send_sem=ss.at[i], recv_sem=rs.at[i],
            device_id=device, device_id_type=MESH,
        )
        copy.start()
        sent.append(copy)
        return copy

    along_z, own_x, rest_x, forwarded, across = {}, {}, {}, {}, {}

    def z_send(k):
        b = buf(k)
        mine = b.at[0, x, c]
        along_z[k] = [send(mine, b.at[4 - d, x, c], z_peers[d - 1]) for d in (1, 3, 2)]

    def own_send(k):
        mine = buf(k).at[0, x, c]
        own_x[k] = [send(mine, mine, to_right), send(mine, mine, to_left)]

    def rest_send(k):
        for copy in along_z[k]:
            copy.wait_recv()
        rest = buf(k).at[pl.ds(1, 3), x, c]
        rest_x[k] = [send(rest, rest, to_right), send(rest, rest, to_left)]
        column = buf(k).at[:, x, c]
        across[k] = [send(column, column, sibling)]

    def own_forward(k):
        own_x[k][0].wait_recv()
        block = buf(k).at[0, left, c]
        forwarded[k] = [send(block, block, to_right)]
        own_x[k][1].wait_recv()

    def rest_forward(k):
        rest_x[k][0].wait_recv()
        block = buf(k).at[1, left, c]
        forwarded[k].append(send(block, block, to_right))
        rest_x[k][1].wait_recv()
        block = buf(k).at[pl.ds(2, 2), right, c]
        forwarded[k].append(send(block, block, to_left))
        for side in (left, right):
            column = buf(k).at[:, side, c]
            across[k].append(send(column, column, sibling))

    def finish(k):
        for copy in forwarded[k]:
            copy.wait_recv()
        last = buf(k).at[:, far, c]
        across[k].append(send(last, last, sibling))
        for copy in across[k]:
            copy.wait_recv()

    def statistics():
        for copy in load_tok:
            copy.wait()

        @pl.loop(0, TOK // 32)
        def _(i):
            rows = pl.ds(pl.multiple_of(i * 32, 32), 32)
            wide = tok[rows, :].astype(jnp.float32)
            mean = jnp.sum(wide * wide, axis=1, keepdims=True) * (1.0 / WIDTH)
            scale[rows, :] = jnp.broadcast_to(lax.rsqrt(mean + 1e-6), (32, HEAD))

    def rotate(field, rows):
        return field * cosv[rows, :] + pltpu.roll(field, HEAD // 2, 1) * sinv[rows, :]

    def row_blocks(step):
        def run(work):
            @pl.loop(0, TOK // step)
            def _(i):
                work(pl.ds(pl.multiple_of(i * step, step), step))
        return run

    pair = []

    def key_or_value():
        for copy in (load_cos, load_sin):
            copy.wait()

        @row_blocks(ROWS)
        def _(rows):
            field = jnp.dot(
                tok[rows, :], wkv[...].reshape(WIDTH, HEAD), preferred_element_type=jnp.float32
            ) * scale[rows, :]
            kv[parity, rows, :] = jnp.where(parity == 0, rotate(field, rows), field).astype(jnp.bfloat16)

        pair.append(send(kv.at[parity], kv.at[parity], y_pair))

    def head_col(zh_, y_, h):
        owner = zh_ * 4 + y_
        slot = mod4(lax.div(owner, 2) - z + 4)
        return pl.multiple_of((slot * 8 + lax.rem(owner, 2) * HEADS + h) * HEAD, HEAD)

    near_heads, far_heads, last_heads = {}, {}, []

    def attend(p):
        @row_blocks(ROWS)
        def _(rows):
            product = jnp.dot(
                tok[rows, :], wq[p].reshape(WIDTH, PAIR), preferred_element_type=jnp.float32
            )
            for h in range(2):
                cols = slice(h * HEAD, (h + 1) * HEAD)
                field = product[:, cols] * scale[rows, :]
                query[rows, cols] = rotate(field, rows).astype(jnp.bfloat16)

        if p == 0:
            pair[0].wait_recv()
        step = 256
        blocks = [(h, i) for h in range(2) for i in range(TOK // step)]
        scores = []
        for h, i in blocks:
            extent = (i + 1) * step
            score = lax.dot_general(
                query[i * step : extent, h * HEAD : (h + 1) * HEAD], kv[0, :extent, :],
                (((1,), (1,)), ((), ())), preferred_element_type=jnp.float32,
            ) * (HEAD ** -0.5)
            q_pos = lax.broadcasted_iota(jnp.int32, (step, extent), 0) + i * step
            k_pos = lax.broadcasted_iota(jnp.int32, (step, extent), 1)
            scores.append(jnp.where(q_pos >= k_pos, score, -1e30))
        parts = []
        for (h, i), score in zip(blocks, scores):
            expo = jnp.exp(score - jnp.max(score, axis=1, keepdims=True))
            total = jnp.sum(expo, axis=1, keepdims=True)
            part = jnp.dot(
                expo.astype(jnp.bfloat16), kv[1, : (i + 1) * step, :],
                preferred_element_type=jnp.float32,
            )
            parts.append((part * (1.0 / total)).astype(jnp.bfloat16))
        for (h, i), part in zip(blocks, parts):
            heads[i * step : (i + 1) * step, pl.ds(head_col(zh, y, 2 * p + h), HEAD)] = part
        block = heads.at[:, pl.ds(head_col(zh, y, 2 * p), PAIR)]
        near_heads[p] = [send(block, block, opposite)]

    def share(p):
        block = heads.at[:, pl.ds(head_col(zh, y, 2 * p), PAIR)]
        near_heads[p] += [send(block, block, peer) for peer in y_peers]

    def relay_heads(p, near):
        pairs_of = (near_heads if near else far_heads)[p]
        first = 1 if near else 0
        side = zh if near else 1 - zh
        for i, (y_, device, half) in enumerate(((mod4(y + 3), y_peers[0], 0), (mod4(y + 1), y_peers[1], 1))):
            pairs_of[first + i].wait_recv()
            rows = pl.ds(half * (TOK // 2), TOK // 2)
            block = heads.at[rows, pl.ds(head_col(side, y_, 2 * p), PAIR)]
            last_heads.append(send(block, block, device))

    def pass_on(p):
        near_heads[p][0].wait_recv()
        block = heads.at[:, pl.ds(head_col(1 - zh, y, 2 * p), PAIR)]
        far_heads[p] = [send(block, block, peer) for peer in y_peers]

    def gather_heads():
        for copy in last_heads:
            copy.wait_recv()

    stores = []

    def output(j):
        cols = pl.ds(j * OUT_COLS, OUT_COLS)

        @row_blocks(ROWS)
        def _(rows):
            product = jnp.dot(
                heads[rows, :], wo[j].reshape(FEATURES, OUT_COLS), preferred_element_type=jnp.float32
            )
            outv[rows, cols] = (res[rows, cols].astype(jnp.float32) + product).astype(jnp.bfloat16)

        store = pltpu.make_async_copy(outv.at[:, cols], out_hbm.at[:, cols], ls.at[CHUNKS + 7 + j])
        store.start()
        stores.append(store)

    own[0].wait()
    z_send(0)
    own_send(0)
    own[1].wait()
    z_send(1)
    own_send(1)
    own[2].wait()
    z_send(2)
    own_send(2)
    for k in range(3, CHUNKS):
        own[k].wait()
        z_send(k)
    statistics()
    own_forward(0)
    rest_send(0)
    own_send(3)
    own_forward(1)
    own_forward(2)
    rest_forward(0)
    own_send(4)
    rest_send(1)
    own_forward(3)
    finish(0)
    key_or_value()
    own_forward(4)
    own_send(5)
    rest_forward(1)
    rest_send(2)
    finish(1)
    attend(0)
    share(0)
    own_send(6)
    own_forward(5)
    rest_forward(2)
    rest_send(3)
    relay_heads(0, True)
    own_forward(6)
    finish(2)
    rest_send(4)
    attend(1)
    share(1)
    rest_forward(3)
    pass_on(0)
    rest_send(5)
    finish(3)
    rest_forward(4)
    rest_send(6)
    relay_heads(0, False)
    relay_heads(1, True)
    finish(4)
    pass_on(1)
    rest_forward(5)
    load_res.wait()
    finish(5)
    relay_heads(1, False)
    rest_forward(6)
    gather_heads()
    output(0)
    output(1)
    output(2)
    finish(6)
    output(3)
    for copy in sent:
        copy.wait_send()
    for store in stores:
        store.wait()


def body(tokens, w_query, w_key, value_weight, w_out):
    cosine, sine = rotary_tables()
    any_space = pl.BlockSpec(memory_space=pl.ANY)
    blocks = (4, 4, 2)
    return pl.pallas_call(
        kernel,
        out_shape=jax.ShapeDtypeStruct((TOK, OUT_COLS * OUT_CHUNKS), jnp.bfloat16),
        in_specs=[any_space] * 7,
        out_specs=any_space,
        scratch_shapes=[
            pltpu.VMEM((TOK, WIDTH), jnp.bfloat16),
            pltpu.VMEM((*blocks, 256, HEAD), jnp.bfloat16),
            pltpu.VMEM((PAIRS, *blocks, 256, PAIR), jnp.bfloat16),
            pltpu.VMEM((OUT_CHUNKS, *blocks, 128, OUT_COLS), jnp.bfloat16),
            pltpu.VMEM((TOK, FEATURES), jnp.bfloat16),
            pltpu.VMEM((TOK, PAIR), jnp.bfloat16),
            pltpu.VMEM((2, TOK, HEAD), jnp.bfloat16),
            pltpu.VMEM((TOK, OUT_COLS * OUT_CHUNKS), jnp.bfloat16),
            pltpu.VMEM((TOK, HEAD), jnp.float32),
            pltpu.VMEM((TOK, HEAD), jnp.float32),
            pltpu.VMEM((TOK, OUT_COLS * OUT_CHUNKS), jnp.bfloat16),
            pltpu.VMEM((TOK, HEAD), jnp.float32),
            pltpu.SemaphoreType.DMA((SEMS,)),
            pltpu.SemaphoreType.DMA((SEMS,)),
            pltpu.SemaphoreType.DMA((CHUNKS + 7 + OUT_CHUNKS,)),
        ],
        compiler_params=pltpu.CompilerParams(
            collective_id=0, has_side_effects=True, vmem_limit_bytes=60 * 2**20
        ),
        cost_estimate=pl.CostEstimate(flops=11 * 10**9, bytes_accessed=12 * 2**20, transcendentals=2**20),
    )(tokens, w_query, w_key, value_weight, w_out, jnp.asarray(cosine), jnp.asarray(sine))


def solution(mesh):
    placed = (P("rep", None), P("rep", "tp"), P("rep", None), P("rep", None), P("rep", "tp"))
    return jax.shard_map(
        body, mesh=mesh, in_specs=placed, out_specs=P("rep", "tp"), check_vma=False
    )
```

time: 129 us -> 121 us (0.938)
  the two profiles are of different devices: /device:TPU:97 before, /device:TPU:1 now
where the time goes in v2:
time: 121 us; the launch traced here: 120 us
  Pallas kernels  118 us (98%)
  local copies, waits for them, and re-layouts  2.26 us (2%)
    pallas_call x1, Pallas kernels, body(): pl.pallas_call(kernel, out_shape=jax.ShapeDtypeStruct((TOK, OUT_COLS * OU...  118 us

profile of v2, /device:TPU:1, one launch (start us, length us, event | category | flops | bytes accessed | tf_op | source)
XLA Modules:
  0.0 120.5 jit_solution(10538908197493978546)
XLA Ops:
  0.0 118.2 %shard_map.73 = bf16[512,1024]{1,0:T(8,128)(2,1)} custom-call(bf16[512,8192]{1,0:T(8,128)(2,1)} %tok_hbm.1, bf16[256,512]{1,0:T(8,128)(2,1)} %wq_hbm.1, bf16[256,512]{1,0:T(8,128)(2,1)} %wk_hbm.1, bf16[256,512]{1,0:T(8,128)(2,1)} %wv_hbm.1, bf16[128,1024]{1,0:T(8,128)(2,1)} %wo_hbm.1, f32[512,128]{1,0:T(8,128)} %constant.4.clone.cos_hbm, ...), custom_call_target="tpu_custom_call" | custom-call | flops 11000000512 | bytes 12582912 | tf_op jit(solution)/shard_map/pallas_call | solution.py:359
  118.2 2.3 %copy.9 = bf16[512,1024]{1,0:T(8,128)(2,1)} copy(bf16[512,1024]{1,0:T(8,128)(2,1)} %shard_map.73) | data formatting | bytes 2097152

commit v3 on v2

--- a/solution.py
+++ b/solution.py
@@ -35,7 +35,7 @@
 
 
 def kernel(tok_hbm, wq_hbm, wk_hbm, wv_hbm, wo_hbm, cos_hbm, sin_hbm, out_hbm,
-           tok, wkv, wq, wo, heads, query, kv, res, cosv, sinv, outv, scale, ss, rs, ls):
+           tok, wkv, wq, wo, heads, query, kv, res, cosv, sinv, outv, total, scale, ss, rs, ls):
     r = lax.axis_index("rep")
     t = lax.axis_index("tp")
     c, x, z = lax.rem(r, 2), lax.rem(lax.div(r, 2), 4), lax.div(r, 8)
@@ -199,12 +199,12 @@
 
         pair.append(send(kv.at[parity], kv.at[parity], y_pair))
 
-    def head_col(zh_, y_, h):
+    def head_index(zh_, y_, p):
         owner = zh_ * 4 + y_
         slot = mod4(lax.div(owner, 2) - z + 4)
-        return pl.multiple_of((slot * 8 + lax.rem(owner, 2) * HEADS + h) * HEAD, HEAD)
-
-    near_heads, far_heads, last_heads = {}, {}, []
+        return slot * 4 + lax.rem(owner, 2) * PAIRS + p
+
+    near_heads, far_heads, last_heads = {}, {}, {}
 
     def attend(p):
         @row_blocks(ROWS)
@@ -234,19 +234,19 @@
         parts = []
         for (h, i), score in zip(blocks, scores):
             expo = jnp.exp(score - jnp.max(score, axis=1, keepdims=True))
-            total = jnp.sum(expo, axis=1, keepdims=True)
+            norm = jnp.sum(expo, axis=1, keepdims=True)
             part = jnp.dot(
                 expo.astype(jnp.bfloat16), kv[1, : (i + 1) * step, :],
                 preferred_element_type=jnp.float32,
             )
-            parts.append((part * (1.0 / total)).astype(jnp.bfloat16))
+            parts.append((part * (1.0 / norm)).astype(jnp.bfloat16))
         for (h, i), part in zip(blocks, parts):
-            heads[i * step : (i + 1) * step, pl.ds(head_col(zh, y, 2 * p + h), HEAD)] = part
-        block = heads.at[:, pl.ds(head_col(zh, y, 2 * p), PAIR)]
+            heads[head_index(zh, y, p), i * step : (i + 1) * step, h * HEAD : (h + 1) * HEAD] = part
+        block = heads.at[head_index(zh, y, p)]
         near_heads[p] = [send(block, block, opposite)]
 
     def share(p):
-        block = heads.at[:, pl.ds(head_col(zh, y, 2 * p), PAIR)]
+        block = heads.at[head_index(zh, y, p)]
         near_heads[p] += [send(block, block, peer) for peer in y_peers]
 
     def relay_heads(p, near):
@@ -256,29 +256,45 @@
         for i, (y_, device, half) in enumerate(((mod4(y + 3), y_peers[0], 0), (mod4(y + 1), y_peers[1], 1))):
             pairs_of[first + i].wait_recv()
             rows = pl.ds(half * (TOK // 2), TOK // 2)
-            block = heads.at[rows, pl.ds(head_col(side, y_, 2 * p), PAIR)]
-            last_heads.append(send(block, block, device))
+            block = heads.at[head_index(side, y_, p), rows]
+            last_heads.setdefault((p, near), []).append(send(block, block, device))
 
     def pass_on(p):
         near_heads[p][0].wait_recv()
-        block = heads.at[:, pl.ds(head_col(1 - zh, y, 2 * p), PAIR)]
+        block = heads.at[head_index(1 - zh, y, p)]
         far_heads[p] = [send(block, block, peer) for peer in y_peers]
 
-    def gather_heads():
-        for copy in last_heads:
-            copy.wait_recv()
+    def gather_heads(*keys):
+        for key in keys:
+            for copy in last_heads[key]:
+                copy.wait_recv()
 
     stores = []
+
+    def times(j, rows, indices):
+        product = None
+        for i in indices:
+            block = wo[j, lax.div(i, 4), lax.rem(i, 4)].reshape(PAIR, OUT_COLS)
+            term = jnp.dot(heads[i, rows, :], block, preferred_element_type=jnp.float32)
+            product = term if product is None else product + term
+        return product
+
+    def output_most(j):
+        cols = pl.ds(j * OUT_COLS, OUT_COLS)
+
+        @row_blocks(ROWS)
+        def _(rows):
+            indices = [head_index(zh_, y_, 0) for zh_ in range(2) for y_ in range(4)]
+            indices += [head_index(zh, y_, 1) for y_ in range(4)]
+            total[rows, cols] = res[rows, cols].astype(jnp.float32) + times(j, rows, indices)
 
     def output(j):
         cols = pl.ds(j * OUT_COLS, OUT_COLS)
 
         @row_blocks(ROWS)
         def _(rows):
-            product = jnp.dot(
-                heads[rows, :], wo[j].reshape(FEATURES, OUT_COLS), preferred_element_type=jnp.float32
-            )
-            outv[rows, cols] = (res[rows, cols].astype(jnp.float32) + product).astype(jnp.bfloat16)
+            indices = [head_index(1 - zh, y_, 1) for y_ in range(4)]
+            outv[rows, cols] = (total[rows, cols] + times(j, rows, indices)).astype(jnp.bfloat16)
 
         store = pltpu.make_async_copy(outv.at[:, cols], out_hbm.at[:, cols], ls.at[CHUNKS + 7 + j])
         store.start()
@@ -287,24 +303,22 @@
     own[0].wait()
     z_send(0)
     own_send(0)
-    own[1].wait()
+    for k in range(1, CHUNKS):
+        own[k].wait()
+    own_send(1)
+    own_send(2)
+    rest_send(0)
     z_send(1)
-    own_send(1)
-    own[2].wait()
-    z_send(2)
-    own_send(2)
-    for k in range(3, CHUNKS):
-        own[k].wait()
-        z_send(k)
-    statistics()
     own_forward(0)
-    rest_send(0)
     own_send(3)
     own_forward(1)
+    statistics()
     own_forward(2)
     rest_forward(0)
     own_send(4)
     rest_send(1)
+    z_send(2)
+    z_send(3)
     own_forward(3)
     finish(0)
     key_or_value()
@@ -312,6 +326,9 @@
     own_send(5)
     rest_forward(1)
     rest_send(2)
+    z_send(4)
+    z_send(5)
+    z_send(6)
     finish(1)
     attend(0)
     share(0)
@@ -338,13 +355,18 @@
     rest_forward(5)
     load_res.wait()
     finish(5)
+    gather_heads((0, True), (0, False), (1, True))
+    output_most(0)
     relay_heads(1, False)
+    output_most(1)
     rest_forward(6)
-    gather_heads()
+    output_most(2)
+    gather_heads((1, False))
     output(0)
     output(1)
     output(2)
     finish(6)
+    output_most(3)
     output(3)
     for copy in sent:
         copy.wait_send()
@@ -366,13 +388,14 @@
             pltpu.VMEM((*blocks, 256, HEAD), jnp.bfloat16),
             pltpu.VMEM((PAIRS, *blocks, 256, PAIR), jnp.bfloat16),
             pltpu.VMEM((OUT_CHUNKS, *blocks, 128, OUT_COLS), jnp.bfloat16),
-            pltpu.VMEM((TOK, FEATURES), jnp.bfloat16),
+            pltpu.VMEM((FEATURES // PAIR, TOK, PAIR), jnp.bfloat16),
             pltpu.VMEM((TOK, PAIR), jnp.bfloat16),
             pltpu.VMEM((2, TOK, HEAD), jnp.bfloat16),
             pltpu.VMEM((TOK, OUT_COLS * OUT_CHUNKS), jnp.bfloat16),
             pltpu.VMEM((TOK, HEAD), jnp.float32),
             pltpu.VMEM((TOK, HEAD), jnp.float32),
             pltpu.VMEM((TOK, OUT_COLS * OUT_CHUNKS), jnp.bfloat16),
+            pltpu.VMEM((TOK, OUT_COLS * OUT_CHUNKS), jnp.float32),
             pltpu.VMEM((TOK, HEAD), jnp.float32),
             pltpu.SemaphoreType.DMA((SEMS,)),
             pltpu.SemaphoreType.DMA((SEMS,)),

time: 121 us -> 117 us (0.967)
  Pallas kernels: 118 us -> 114 us
    pallas_call x1, Pallas kernels: 118 us -> 114 us  [body(): pl.pallas_call(kernel, out_shape=jax.ShapeDtypeStruct((TOK, OUT_COLS * OU...]
where the time goes in v3:
time: 117 us; the launch traced here: 116 us
  Pallas kernels  114 us (97%)
  local copies, waits for them, and re-layouts  2.26 us (2%)
    pallas_call x1, Pallas kernels, body(): pl.pallas_call(kernel, out_shape=jax.ShapeDtypeStruct((TOK, OUT_COLS * OU...  114 us

profile of v3, /device:TPU:1, one launch (start us, length us, event | category | flops | bytes accessed | tf_op | source)
XLA Modules:
  0.0 116.4 jit_solution(12909035732745162768)
XLA Ops:
  0.0 114.1 %shard_map.73 = bf16[512,1024]{1,0:T(8,128)(2,1)} custom-call(bf16[512,8192]{1,0:T(8,128)(2,1)} %tok_hbm.1, bf16[256,512]{1,0:T(8,128)(2,1)} %wq_hbm.1, bf16[256,512]{1,0:T(8,128)(2,1)} %wk_hbm.1, bf16[256,512]{1,0:T(8,128)(2,1)} %wv_hbm.1, bf16[128,1024]{1,0:T(8,128)(2,1)} %wo_hbm.1, f32[512,128]{1,0:T(8,128)} %constant.4.clone.cos_hbm, ...), custom_call_target="tpu_custom_call" | custom-call | flops 11000000512 | bytes 12582912 | tf_op jit(solution)/shard_map/pallas_call | solution.py:381
  114.1 2.3 %copy.9 = bf16[512,1024]{1,0:T(8,128)(2,1)} copy(bf16[512,1024]{1,0:T(8,128)(2,1)} %shard_map.73) | data formatting | bytes 2097152

commit v4 on v3

--- a/solution.py
+++ b/solution.py
@@ -19,7 +19,7 @@
 PAIR = 2 * HEAD
 PAIRS = HEADS // 2
 CHUNKS = 1 + PAIRS + OUT_CHUNKS
-ROWS = 128
+ROWS = 256
 SEMS = 160
 
 

time: 117 us -> 115 us (0.983)
  Pallas kernels: 114 us -> 112 us
    pallas_call x1, Pallas kernels: 114 us -> 112 us  [body(): pl.pallas_call(kernel, out_shape=jax.ShapeDtypeStruct((TOK, OUT_COLS * OU...]
where the time goes in v4:
time: 115 us
  Pallas kernels  112 us (97%)
  local copies, waits for them, and re-layouts  2.26 us (2%)
    pallas_call x1, Pallas kernels, body(): pl.pallas_call(kernel, out_shape=jax.ShapeDtypeStruct((TOK, OUT_COLS * OU...  112 us

profile of v4, /device:TPU:1, one launch (start us, length us, event | category | flops | bytes accessed | tf_op | source)
XLA Modules:
  0.0 114.7 jit_solution(16145174602523715467)
XLA Ops:
  0.0 112.4 %shard_map.73 = bf16[512,1024]{1,0:T(8,128)(2,1)} custom-call(bf16[512,8192]{1,0:T(8,128)(2,1)} %tok_hbm.1, bf16[256,512]{1,0:T(8,128)(2,1)} %wq_hbm.1, bf16[256,512]{1,0:T(8,128)(2,1)} %wk_hbm.1, bf16[256,512]{1,0:T(8,128)(2,1)} %wv_hbm.1, bf16[128,1024]{1,0:T(8,128)(2,1)} %wo_hbm.1, f32[512,128]{1,0:T(8,128)} %constant.4.clone.cos_hbm, ...), custom_call_target="tpu_custom_call" | custom-call | flops 11000000512 | bytes 12582912 | tf_op jit(solution)/shard_map/pallas_call | solution.py:381
  112.4 2.3 %copy.9 = bf16[512,1024]{1,0:T(8,128)(2,1)} copy(bf16[512,1024]{1,0:T(8,128)(2,1)} %shard_map.73) | data formatting | bytes 2097152

commit v5 on v4

--- a/solution.py
+++ b/solution.py
@@ -361,6 +361,9 @@
     output_most(1)
     rest_forward(6)
     output_most(2)
+    early = len(sent) - 16
+    for copy in sent[:early]:
+        copy.wait_send()
     gather_heads((1, False))
     output(0)
     output(1)
@@ -368,7 +371,7 @@
     finish(6)
     output_most(3)
     output(3)
-    for copy in sent:
+    for copy in sent[early:]:
         copy.wait_send()
     for store in stores:
         store.wait()

time: 115 us -> 115 us (level)
  no operation moved by 1% of the time
where the time goes in v5:
time: 115 us
  Pallas kernels  112 us (97%)
  local copies, waits for them, and re-layouts  2.26 us (2%)
    pallas_call x1, Pallas kernels, body(): pl.pallas_call(kernel, out_shape=jax.ShapeDtypeStruct((TOK, OUT_COLS * OU...  112 us

profile of v5, /device:TPU:1, one launch (start us, length us, event | category | flops | bytes accessed | tf_op | source)
XLA Modules:
  0.0 114.7 jit_solution(9825194373066604803)
XLA Ops:
  0.0 112.4 %shard_map.73 = bf16[512,1024]{1,0:T(8,128)(2,1)} custom-call(bf16[512,8192]{1,0:T(8,128)(2,1)} %tok_hbm.1, bf16[256,512]{1,0:T(8,128)(2,1)} %wq_hbm.1, bf16[256,512]{1,0:T(8,128)(2,1)} %wk_hbm.1, bf16[256,512]{1,0:T(8,128)(2,1)} %wv_hbm.1, bf16[128,1024]{1,0:T(8,128)(2,1)} %wo_hbm.1, f32[512,128]{1,0:T(8,128)} %constant.4.clone.cos_hbm, ...), custom_call_target="tpu_custom_call" | custom-call | flops 11000000512 | bytes 12582912 | tf_op jit(solution)/shard_map/pallas_call | solution.py:384
  112.4 2.3 %copy.9 = bf16[512,1024]{1,0:T(8,128)(2,1)} copy(bf16[512,1024]{1,0:T(8,128)(2,1)} %shard_map.73) | data formatting | bytes 2097152
